TPU v7x, 1024 devices: a whole 4x8x16 slice. The times are simulated.
1024 devices in a mesh: ga: 128 (over y, z), band: 8 (over x, core).
Axes of the slice: x: 4, y: 8, z: 16, core: 2. Of those that a mesh axis runs over, the one named last changes fastest.
Arguments:
- band_coeffs: bfloat16 [131072, 512], P('ga', 'band'), may hold values from -6 to 6
- beta_vectors: bfloat16 [131072, 2048], P('ga'), may hold values from -0.015625 to 0.015625
- atomic_waves: bfloat16 [131072, 1280], P('ga'), may hold values from -0.015625 to 0.015625
- beta_coupling: float32 [2048, 11], replicated, may hold values from -1 to 2
- ortho_inverse: bfloat16 [1280, 1280], replicated, may hold values from -1 to 2
- hubbard_energy: float32 [3], replicated, may hold values from 1 to 4
- band_weight: float32 [512], P('band'), may hold values from 0 to 0.0078125
- orbital_start: int32 [1280], replicated, may hold values from 0 to 1277, as said below
- orbital_species: int32 [1280], replicated, may hold values from 0 to 2, as said below
- beta_start: int32 [2048], replicated, may hold values from 0 to 2046, as said below
Outputs:
- hubbard_apply: bfloat16 [131072, 512], P('ga', 'band')
Inputs may be any that keep to these rules, and one draw needn't show every extreme that they name: `orbital_start`: every atom holds 3 or 5 consecutive orbitals; each orbital holds the index of its atom's first orbital. `orbital_species`: orbitals of 5-orbital atoms have species 0 or 1, orbitals of 3-orbital atoms species 2. `beta_start`: every atom holds 2 or 6 consecutive projectors; each projector holds the index of its atom's first projector.
All inputs are finite; a program needn't handle non-finite values.
Results may differ from a plain program's by a relative error of at most 0.0085.
Values sent between devices are 32-bit elements; how exact they have to be, the bound alone decides.
A program may use at most 32 MiB of HBM per device.

v0:
```python
import jax
import jax.numpy as jnp
from jax import lax
from jax.sharding import PartitionSpec as P

ORB_REACH = 4
BETA_REACH = 5
NSPEC = 3


def rim_shift(extended, reach, offset, rows):
    return lax.slice_in_dim(extended, reach + offset, reach + offset + rows, axis=0)


def same_atom(start_ext, reach, rows):
    centre = rim_shift(start_ext, reach, 0, rows)
    return jnp.stack(
        [
            (rim_shift(start_ext, reach, offset, rows) == centre).astype(jnp.float32)
            for offset in range(-reach, reach + 1)
        ]
    )


def band_apply(coupling, extended, reach, rows):
    total = jnp.zeros((rows, extended.shape[1]), jnp.float32)
    for offset in range(-reach, reach + 1):
        total = total + coupling[offset + reach][:, None] * rim_shift(extended, reach, offset, rows)
    return total


def beta_matrix(beta_coupling, beta_start):
    rows = beta_start.shape[0]
    start_ext = jnp.pad(beta_start, BETA_REACH, constant_values=-1)
    mask = same_atom(start_ext, BETA_REACH, rows)
    padded = jnp.pad(beta_coupling, ((BETA_REACH, BETA_REACH), (0, 0)))
    terms = []
    for offset in range(-BETA_REACH, BETA_REACH + 1):
        mirror = rim_shift(padded, BETA_REACH, offset, rows)[:, BETA_REACH - offset]
        terms.append(0.5 * (beta_coupling[:, BETA_REACH + offset] + mirror))
    return jnp.stack(terms) * mask


def occupancy(extended, weights, mask, reach, rows):
    centre = rim_shift(extended, reach, 0, rows)
    weighted = centre * weights[None, :]
    return (
        jnp.stack(
            [
                jnp.sum(weighted * rim_shift(extended, reach, offset, rows), axis=1)
                for offset in range(-reach, reach + 1)
            ]
        )
        * mask
    )


def hubbard_mix(occupied, u_rows, mask, extended, reach, rows):
    centre_flag = (jnp.arange(2 * reach + 1) == reach).astype(jnp.float32)[:, None]
    potential = u_rows[None, :] * (0.5 * centre_flag - occupied) * mask
    return band_apply(potential, extended, reach, rows)


def per_orbital_u(species, hubbard_energy):
    onehot = (species[:, None] == jnp.arange(NSPEC)[None, :]).astype(jnp.float32)
    return jnp.dot(onehot, hubbard_energy, precision=lax.Precision.HIGHEST)


def shards(
    band_coeffs,
    beta_vectors,
    atomic_waves,
    beta_coupling,
    ortho_inverse,
    hubbard_energy,
    band_weight,
    orbital_start,
    orbital_species,
    beta_start,
):
    highest = lax.Precision.HIGHEST
    nbeta = beta_vectors.shape[1]
    norbit = atomic_waves.shape[1]
    coupling = beta_matrix(beta_coupling, beta_start)
    beta_correlation = lax.psum(
        jnp.dot(beta_vectors.T, band_coeffs, preferred_element_type=jnp.float32), "ga"
    )
    corrected = band_apply(
        coupling, jnp.pad(beta_correlation, ((BETA_REACH, BETA_REACH), (0, 0))), BETA_REACH, nbeta
    ).astype(jnp.bfloat16)
    correlation_psi = (
        band_coeffs.astype(jnp.float32)
        + jnp.dot(beta_vectors, corrected, preferred_element_type=jnp.float32)
    ).astype(jnp.bfloat16)
    partial_value = jnp.dot(atomic_waves.T, correlation_psi, preferred_element_type=jnp.float32)
    u_full = per_orbital_u(orbital_species, hubbard_energy)
    start_full = jnp.pad(orbital_start, ORB_REACH, constant_values=-1)
    ortho_full = ortho_inverse.astype(jnp.float32)
    summed = lax.psum(partial_value, "ga")
    projections = jnp.dot(ortho_full, summed, precision=highest)
    extended = jnp.pad(projections, ((ORB_REACH, ORB_REACH), (0, 0)))
    mask = same_atom(start_full, ORB_REACH, norbit)
    occupied = lax.psum(occupancy(extended, band_weight, mask, ORB_REACH, norbit), "band")
    mixed = hubbard_mix(occupied, u_full, mask, extended, ORB_REACH, norbit)
    rotated = jnp.dot(ortho_full, mixed, precision=highest)
    rotated_half = rotated.astype(jnp.bfloat16)
    hubbard_waves = jnp.dot(atomic_waves, rotated_half, preferred_element_type=jnp.float32)
    wave_half = hubbard_waves.astype(jnp.bfloat16)
    beta_update = lax.psum(
        jnp.dot(beta_vectors.T, wave_half, preferred_element_type=jnp.float32), "ga"
    )
    correction = band_apply(
        coupling, jnp.pad(beta_update, ((BETA_REACH, BETA_REACH), (0, 0))), BETA_REACH, nbeta
    ).astype(jnp.bfloat16)
    return (
        hubbard_waves + jnp.dot(beta_vectors, correction, preferred_element_type=jnp.float32)
    ).astype(jnp.bfloat16)


def solution(mesh):
    placed = (
        P("ga", "band"),
        P("ga", None),
        P("ga", None),
        P(),
        P(),
        P(),
        P("band"),
        P(),
        P(),
        P(),
    )
    return jax.shard_map(
        shards, mesh=mesh, in_specs=placed, out_specs=P("ga", "band"), check_vma=False
    )
```

profile of v0, /device:TPU:6, one launch (start us, length us, event | category | flops | bytes accessed | tf_op | source)
XLA Modules:
  0.0 893.5 jit_solution(16101456095081056845)
XLA Ops:
  6.5 0.0 copy-start
  6.5 0.0 copy-start.3
  6.5 0.0 copy-start.14
  6.5 0.0 all-reduce.10.cloned.1.call-start
  6.5 4.1 fusion.134
  10.6 0.0 all-reduce.10.cloned.1.call-update
  10.6 0.0 all-reduce.12.cloned.1.call-start
  10.7 0.0 copy-done.3
  10.7 0.1 multiply_bitcast_fusion.8
  10.8 0.9 multiply_bitcast_fusion
  11.6 0.0 copy-done.14
  11.6 0.1 fusion.117
  11.7 0.2 stack.181
  11.9 1.7 stack.160
  13.6 0.1 fusion.132
  13.7 0.0 copy-start.5
  13.7 0.0 copy-start.6
  13.7 0.0 copy-start.7
  13.7 0.0 copy-start.8
  13.7 0.0 copy-start.9
  13.7 0.0 copy-start.10
  13.7 0.0 copy-start.11
  13.7 0.0 copy-start.12
  13.7 0.0 copy-start.13
  13.7 281.0 %all-reduce.10.cloned.1.call-done = f32[2048,64]{0,1:T(8,128)} async-done(((f32[2048,64]{0,1:T(8,128)}), f32[2048,64]{0,1:T(8,128)}) %all-reduce.10.cloned.1.call-update) | async-done | bytes 524304 | tf_op jit(solution)/shard_map/psum | solution.py:85
  294.8 0.0 copy-start.4
  294.8 8.8 convolution_bitcast_fusion.2
  303.6 0.0 copy-done.5
  303.6 0.0 copy-done.6
  303.6 0.0 copy-done.7
  303.6 0.0 copy-done.8
  303.6 0.0 copy-done.9
  303.6 0.0 copy-done.10
  303.6 0.0 copy-done.11
  303.6 0.0 copy-done.12
  303.6 0.0 copy-done.13
  303.6 0.0 copy-start.15
  303.7 0.0 all-reduce.12.cloned.1.call-update
  303.7 0.0 all-reduce.14.cloned.1.call-start
  303.7 0.0 copy-done.4
  303.7 0.1 fusion.116
  303.9 0.1 stack.208
  304.0 0.0 copy-done.16
  304.1 0.0 copy-done.17
  304.1 0.5 convolution_reduce_fusion
  304.6 264.9 %all-reduce.12.cloned.1.call-done = f32[1280,64]{0,1:T(8,128)} async-done(((f32[1280,64]{0,1:T(8,128)}), f32[1280,64]{0,1:T(8,128)}) %all-reduce.12.cloned.1.call-update) | async-done | bytes 327696 | tf_op jit(solution)/shard_map/psum | solution.py:99
  569.6 0.0 copy-done
  569.6 4.0 convolution_bitcast_fusion.1
  573.6 0.0 copy-start.2
  573.6 0.7 copy-done.2
  574.3 0.0 copy-done.15
  574.3 0.8 fusion.26
  575.2 0.1 stack.191
  575.3 21.6 %psum.30 = f32[9,1280]{1,0:T(8,128)S(1)} all-reduce(f32[9,1280]{1,0:T(8,128)S(1)} %mul.535), channel_id=1, replica_groups=mesh['ga'=128,'band'=8] {'band'}, use_global_device_ids=true, to_apply=%region_11.12 | all-reduce | flops 11520 | bytes 92160 | tf_op jit(solution)/shard_map/psum | solution.py:103
  596.9 0.0 copy-start.1
  596.9 0.1 multiply_multiply_fusion.9
  597.0 0.1 slice_reduce_fusion.8
  597.2 5.8 convolution_convert_fusion
  603.0 2.6 fusion.133
  605.6 0.0 copy-done.1
  605.6 1.7 convolution_bitcast_fusion
  607.3 0.0 all-reduce.14.cloned.1.call-update
  607.3 272.2 %all-reduce.14.cloned.1.call-done = f32[2048,64]{0,1:T(8,128)} async-done(((f32[2048,64]{0,1:T(8,128)}), f32[2048,64]{0,1:T(8,128)}) %all-reduce.14.cloned.1.call-update) | async-done | bytes 524304 | tf_op jit(solution)/shard_map/psum | solution.py:109
  879.5 7.5 fusion.3
  (24 shorter events, 0.1 us)
Async XLA Ops:
  6.5 563.0 %copy-start = (bf16[1280,1280]{1,0:T(8,128)(2,1)S(1)}, bf16[1280,1280]{1,0:T(8,128)(2,1)}, u32[]{:S(2)}) copy-start(bf16[1280,1280]{1,0:T(8,128)(2,1)} %param.14) | copy-start | bytes 9830404
  6.5 4.1 copy-start.3
  6.5 5.1 copy-start.14
  6.5 288.2 %all-reduce.10.cloned.1.call-start = ((), (), s32[]{:S(2)}) async-start(), calls=%async_computation | async-start | bytes 1048576 | tf_op jit(solution)/shard_map/psum | solution.py:85
  10.6 558.9 %all-reduce.12.cloned.1.call-start = ((), (), s32[]{:S(2)}) async-start(), calls=%async_computation.1 | async-start | bytes 655360 | tf_op jit(solution)/shard_map/psum | solution.py:99
  13.7 289.9 %copy-start.5 = (f32[1,2048]{1,0:T(1,128)}, f32[1,2048]{1,0:T(1,128)S(1)}, u32[]{:S(2)}) copy-start(f32[1,2048]{1,0:T(1,128)S(1)} %get-tuple-element.25) | copy-start | bytes 24580
  13.7 289.9 %copy-start.6 = (f32[1,2048]{1,0:T(1,128)}, f32[1,2048]{1,0:T(1,128)S(1)}, u32[]{:S(2)}) copy-start(f32[1,2048]{1,0:T(1,128)S(1)} %get-tuple-element.26) | copy-start | bytes 24580
  13.7 289.9 %copy-start.7 = (f32[1,2048]{1,0:T(1,128)}, f32[1,2048]{1,0:T(1,128)S(1)}, u32[]{:S(2)}) copy-start(f32[1,2048]{1,0:T(1,128)S(1)} %get-tuple-element.27) | copy-start | bytes 24580
  13.7 289.9 %copy-start.8 = (f32[1,2048]{1,0:T(1,128)}, f32[1,2048]{1,0:T(1,128)S(1)}, u32[]{:S(2)}) copy-start(f32[1,2048]{1,0:T(1,128)S(1)} %get-tuple-element.28) | copy-start | bytes 24580
  13.7 289.9 %copy-start.9 = (f32[1,2048]{1,0:T(1,128)}, f32[1,2048]{1,0:T(1,128)S(1)}, u32[]{:S(2)}) copy-start(f32[1,2048]{1,0:T(1,128)S(1)} %get-tuple-element.29) | copy-start | bytes 24580
  13.7 289.9 %copy-start.10 = (f32[1,2048]{1,0:T(1,128)}, f32[1,2048]{1,0:T(1,128)S(1)}, u32[]{:S(2)}) copy-start(f32[1,2048]{1,0:T(1,128)S(1)} %get-tuple-element.30) | copy-start | bytes 24580
  13.7 289.9 %copy-start.11 = (f32[1,2048]{1,0:T(1,128)}, f32[1,2048]{1,0:T(1,128)S(1)}, u32[]{:S(2)}) copy-start(f32[1,2048]{1,0:T(1,128)S(1)} %get-tuple-element.31) | copy-start | bytes 24580
  13.7 289.9 %copy-start.12 = (f32[1,2048]{1,0:T(1,128)}, f32[1,2048]{1,0:T(1,128)S(1)}, u32[]{:S(2)}) copy-start(f32[1,2048]{1,0:T(1,128)S(1)} %get-tuple-element.32) | copy-start | bytes 24580
  13.7 289.9 %copy-start.13 = (f32[1,2048]{1,0:T(1,128)}, f32[1,2048]{1,0:T(1,128)S(1)}, u32[]{:S(2)}) copy-start(f32[1,2048]{1,0:T(1,128)S(1)} %get-tuple-element.33) | copy-start | bytes 24580
  294.8 8.9 %copy-start.4 = (s32[1280]{0:T(1024)S(1)}, s32[1280]{0:T(1024)}, u32[]{:S(2)}) copy-start(s32[1280]{0:T(1024)} %param.17) | copy-start | bytes 15364
  294.8 9.3 %copy-start.16 = (s32[1280]{0:T(1024)S(1)}, s32[1280]{0:T(1024)}, u32[]{:S(2)}) copy-start(s32[1280]{0:T(1024)} %param.18) | copy-start | bytes 15364
  294.8 9.3 %copy-start.17 = (f32[3]{0:T(128)S(1)}, f32[3]{0:T(128)}, u32[]{:S(2)}) copy-start(f32[3]{0:T(128)} %param.15) | copy-start | bytes 40
  303.6 270.7 %copy-start.15 = (f32[64]{0:T(128)S(1)}, f32[64]{0:T(128)}, u32[]{:S(2)}) copy-start(f32[64]{0:T(128)} %param.16) | copy-start | bytes 772
  303.7 575.8 %all-reduce.14.cloned.1.call-start = ((), (), s32[]{:S(2)}) async-start(), calls=%async_computation.2 | async-start | bytes 1048576 | tf_op jit(solution)/shard_map/psum | solution.py:109
  573.6 0.7 copy-start.2
  596.9 8.7 copy-start.1
Sparse Core Ops, SparseCore 0:
  10.8 283.9 all-reduce.9
  303.8 265.7 all-reduce.11
  607.4 272.0 all-reduce.13
where the time goes:
time: 894 us
  waiting for transfers between devices  818 us (91%)
  matrix products  35 us (4%)
  blocking collectives  21.6 us (2%)
  between operations  13.6 us (2%)
    psum x1, waiting for transfers between devices, shards(): lax.psum(jnp.dot(beta_vectors.T, band_coeffs, preferred_element_type=jnp....  281 us
    psum x1, waiting for transfers between devices, shards(): lax.psum(jnp.dot(beta_vectors.T, wave_half, preferred_element_type=jnp.fl...  272 us
    psum x1, waiting for transfers between devices, shards(): summed = lax.psum(partial_value, 'ga')  265 us
    psum x1, blocking collectives, shards(): lax.psum(occupancy(extended, band_weight, mask, ORB_REACH, norbit), 'band')  21.6 us
  transfers between devices with their start and end apart: 3, of which 3 were waited for; matrix products, arithmetic and copies ran while one was open for 0% of the time, Pallas kernels for 0%

commit v1 on v0

v1 whole, which is shorter than its diff:
```python
import functools

import jax
import jax.numpy as jnp
from jax import lax
from jax.experimental import pallas as pl
from jax.experimental.pallas import tpu as pltpu
from jax.sharding import PartitionSpec as P

ORB_REACH = 4
BETA_REACH = 5
NY = 8
NZ = 16
HALVES = 1
MESH = pl.DeviceIdType.MESH
F32 = jnp.float32
BF16 = jnp.bfloat16


def dot_nn(a, b):
    return jnp.dot(a, b, preferred_element_type=F32)


def dot_nt(a, b):
    return lax.dot_general(a, b, (((1,), (1,)), ((), ())), preferred_element_type=F32)


def ahead(x, k):
    n = x.shape[1]
    return x if k % n == 0 else pltpu.roll(x, (-k) % n, 1)


def order(n):
    return sorted(range(1, n), key=lambda d: -min(d, n - d))


def wait_bytes(ref, sem):
    pltpu.make_async_copy(ref, ref, sem).wait()


class RingSum:
    def __init__(self, src, dst, row0, rows, y_in, z_in, mine, recv, send, y, z, band):
        self.src, self.dst = src, dst
        self.lanes = src.shape[1]
        self.split = NY * 8 // rows
        self.width = self.lanes // self.split
        self.tiles = self.width // 128
        self.stride = NZ // self.tiles
        self.row0 = row0
        self.y_in, self.z_in, self.mine = y_in, z_in, mine
        self.recv, self.send = recv, send
        self.y, self.z, self.band = y, z, band

    def rows_of(self, y):
        return pl.ds(pl.multiple_of(self.row0 + (y // self.split) * 8, 8), 8)

    def lanes_of(self, y):
        if self.split == 1:
            return pl.ds(0, self.width)
        return pl.ds(pl.multiple_of((y % self.split) * self.width, 128), self.width)

    def tile_lanes(self, y, tile):
        base = (y % self.split) * self.width if self.split > 1 else 0
        return pl.ds(pl.multiple_of(base + tile * 128, 128), 128)

    def owns(self, z):
        ok = z // self.stride < self.tiles
        if self.stride > 1:
            ok = jnp.logical_and(ok, z % self.stride == 0)
        return ok

    def all_own(self):
        return self.tiles == NZ

    def copy(self, src, dst, phase, y, z):
        pltpu.make_async_remote_copy(
            src_ref=src,
            dst_ref=dst,
            send_sem=self.send.at[phase],
            recv_sem=self.recv.at[phase],
            device_id=(y * NZ + z, self.band),
            device_id_type=MESH,
        ).start()

    def start(self):
        for d in order(NY):
            to = (self.y + d) % NY
            self.copy(self.src.at[self.rows_of(to), self.lanes_of(to)], self.y_in.at[d - 1], 0, to, self.z)

    def when(self, cond, body):
        if self.all_own():
            body()
        else:
            pl.when(cond)(body)

    def second(self):
        wait_bytes(self.y_in, self.recv.at[0])
        total = self.src[self.rows_of(self.y), self.lanes_of(self.y)]
        for d in range(NY - 1):
            total = total + self.y_in[d]
        self.mine[...] = total
        for d in order(NZ):
            to = (self.z + d) % NZ
            tile = to // self.stride

            def go(to=to, tile=tile, d=d):
                lanes = pl.ds(pl.multiple_of(tile * 128, 128), 128)
                self.copy(self.mine.at[:, lanes], self.z_in.at[d - 1], 1, self.y, to)

            self.when(self.owns(to), go)

    def third(self):
        def go():
            wait_bytes(self.z_in, self.recv.at[1])
            tile = self.z // self.stride
            total = self.mine[:, pl.ds(pl.multiple_of(tile * 128, 128), 128)]
            for d in range(NZ - 1):
                total = total + self.z_in[d]
            here = (self.rows_of(self.y), self.tile_lanes(self.y, tile))
            self.dst[here] = total
            for d in order(NZ):
                to = (self.z + d) % NZ
                self.copy(self.dst.at[here], self.dst.at[here], 2, self.y, to)

        self.when(self.owns(self.z), go)

    def z_wait(self, sem):
        if self.all_own():
            wait_bytes(self.z_in, sem)
        else:
            own = self.owns(self.z)
            pl.when(own)(lambda: wait_bytes(self.z_in.at[pl.ds(0, self.tiles - 1)], sem))
            pl.when(jnp.logical_not(own))(lambda: wait_bytes(self.z_in.at[pl.ds(0, self.tiles)], sem))

    def fourth(self):
        self.z_wait(self.recv.at[2])
        here = (self.rows_of(self.y), self.lanes_of(self.y))
        for d in order(NY):
            to = (self.y + d) % NY
            self.copy(self.dst.at[here], self.dst.at[here], 3, to, self.z)

    def finish(self):
        wait_bytes(self.y_in, self.recv.at[3])

    def drain(self):
        wait_bytes(self.y_in, self.send.at[0])
        self.z_wait(self.send.at[1])
        self.when(self.owns(self.z), lambda: wait_bytes(self.z_in, self.send.at[2]))
        wait_bytes(self.y_in, self.send.at[3])


def split3(x):
    high = x.astype(BF16)
    rest = x - high.astype(F32)
    mid = rest.astype(BF16)
    low = (rest - mid.astype(F32)).astype(BF16)
    return jnp.concatenate([high, mid, low], axis=0)


def kernel(
    psi_hbm, beta_hbm, atom_hbm, ortho_hbm, coup_in, energy, weight_in, ostart, ospec, bstart, out,
    psi, beta, atom, ortho, coup, orb, wcol, wb, wo, fb, fo, half_b, half_o, hw, cpsi, pot,
    occ_mine, occ_in, yb_in, yo_in, z_in, mine_b, mine_o, load_sem, recv, send, occ_sem,
):
    bands, npw = psi.shape
    nbeta, norb = beta.shape[1], atom.shape[1]
    rows = bands // HALVES
    g = lax.axis_index("ga")
    band = lax.axis_index("band")
    y, z = g // NZ, g % NZ
    nband = 8
    step = 512

    loads = [pltpu.make_async_copy(psi_hbm, psi, load_sem.at[0])]
    for j in range(nbeta // step):
        cols = pl.ds(j * step, step)
        loads.append(pltpu.make_async_copy(beta_hbm.at[:, cols], beta.at[:, cols], load_sem.at[1 + j]))
    late = [
        pltpu.make_async_copy(atom_hbm, atom, load_sem.at[5]),
        pltpu.make_async_copy(ortho_hbm, ortho, load_sem.at[6]),
    ]
    for c in loads + late:
        c.start()

    barrier = pltpu.get_barrier_semaphore()
    for d in order(NZ):
        pl.semaphore_signal(barrier, inc=1, device_id=(y * NZ + (z + d) % NZ, band), device_id_type=MESH)
    for d in order(NY):
        pl.semaphore_signal(barrier, inc=1, device_id=(((y + d) % NY) * NZ + z, band), device_id_type=MESH)
    for d in range(1, nband):
        pl.semaphore_signal(barrier, inc=1, device_id=(g, (band + d) % nband), device_id_type=MESH)

    def ring(which, h):
        i = which * HALVES + h
        if which == 1:
            src, dst, y_in, mine = wo, fo, yo_in.at[h], mine_o.at[h]
        else:
            n = (which // 2) * HALVES + h
            src, dst, y_in, mine = wb.at[which // 2], fb.at[which // 2], yb_in.at[n], mine_b.at[n]
        return RingSum(src, dst, h * rows, rows, y_in, z_in.at[i], mine, recv.at[i], send.at[i], y, z, band)

    sums = [[ring(w, h) for h in range(HALVES)] for w in range(3)]
    halves = range(HALVES)
    part = [pl.ds(h * rows, rows) for h in halves]

    loads[0].wait()
    for h in halves:
        for j in range(nbeta // step):
            if h == 0:
                loads[1 + j].wait()
            cols = pl.ds(j * step, step)
            wb[0, part[h], cols] = dot_nn(psi[part[h], :], beta[:, cols])
        if h == 0:
            pl.semaphore_wait(barrier, NZ - 1 + NY - 1 + nband - 1)
        sums[0][h].start()

    place = lax.broadcasted_iota(jnp.int32, (1, nbeta), 1)
    first = bstart[...]
    for k in range(-BETA_REACH, BETA_REACH + 1):
        there = jnp.logical_and(place + k >= 0, place + k < nbeta)
        same = jnp.logical_and(ahead(first, k) == first, there)
        mirror = ahead(coup_in[BETA_REACH - k : BETA_REACH - k + 1, :], k)
        value = 0.5 * (coup_in[BETA_REACH + k : BETA_REACH + k + 1, :] + mirror)
        coup[BETA_REACH + k : BETA_REACH + k + 1, :] = jnp.where(same, value, 0.0)
    place = lax.broadcasted_iota(jnp.int32, (1, norb), 1)
    first = ostart[...]
    for k in range(-ORB_REACH, ORB_REACH + 1):
        there = jnp.logical_and(place + k >= 0, place + k < norb)
        same = jnp.logical_and(ahead(first, k) == first, there)
        orb[ORB_REACH + k : ORB_REACH + k + 1, :] = jnp.where(same, 1.0, 0.0)
    species = ospec[...]
    u = jnp.zeros((1, norb), F32)
    for s in range(3):
        u = u + jnp.where(species == s, energy[0, s], 0.0)
    orb[2 * ORB_REACH + 1 : 2 * ORB_REACH + 2, :] = u
    row = lax.broadcasted_iota(jnp.int32, (bands, bands), 0)
    col = lax.broadcasted_iota(jnp.int32, (bands, bands), 1)
    wcol[...] = jnp.sum(jnp.where(row == col, weight_in[...], 0.0), axis=1, keepdims=True)

    def apply_q(full, h):
        for i in range(rows // 16):
            pair = []
            for j in range(2):
                x = full[h * rows + i * 16 + j * 8 : h * rows + i * 16 + j * 8 + 8, :]
                total = coup[BETA_REACH : BETA_REACH + 1, :] * x
                for k in range(-BETA_REACH, BETA_REACH + 1):
                    if k != 0:
                        total = total + coup[BETA_REACH + k : BETA_REACH + k + 1, :] * ahead(x, k)
                pair.append(total)
            half_b[h * rows + i * 16 : h * rows + i * 16 + 16, :] = jnp.concatenate(pair, axis=0).astype(BF16)

    block = 256

    def middle(which):
        for name in ("second", "third", "fourth"):
            for h in halves:
                getattr(sums[which][h], name)()

    middle(0)
    for c in late:
        c.wait()
    for h in halves:
        sums[0][h].finish()
        apply_q(fb.at[0], h)
        for j in range(npw // block):
            cols = pl.ds(j * block, block)
            value = psi[part[h], cols].astype(F32) + dot_nt(half_b[part[h], :], beta[cols, :])
            cpsi[part[h], cols] = value.astype(BF16)
        for j in range(norb // block):
            cols = pl.ds(j * block, block)
            wo[part[h], cols] = dot_nn(cpsi[part[h], :], atom[:, cols])
        sums[1][h].start()

    middle(1)

    def times_ortho(x, h):
        stacked = split3(x)
        for j in range(norb // block):
            cols = pl.ds(j * block, block)
            y3 = dot_nt(stacked, ortho[cols, :])
            yield cols, y3[:rows] + y3[rows : 2 * rows] + y3[2 * rows :]

    accs = None
    for h in halves:
        sums[1][h].finish()
        for cols, value in times_ortho(fo[part[h], :], h):
            wo_proj = value
            pot[part[h], cols] = wo_proj
    for i in range(bands // 8):
        p = pot[i * 8 : i * 8 + 8, :]
        weighted = p * wcol[i * 8 : i * 8 + 8, :]
        terms = [weighted * ahead(p, k) for k in range(ORB_REACH + 1)]
        accs = terms if accs is None else [a + t for a, t in zip(accs, terms)]
    for k in range(ORB_REACH + 1):
        occ_mine[k : k + 1, :] = jnp.sum(accs[k], axis=0, keepdims=True)
    occ_mine[ORB_REACH + 1 :, :] = jnp.zeros((8 - ORB_REACH - 1, norb), F32)
    for d in range(1, nband):
        pltpu.make_async_remote_copy(
            src_ref=occ_mine,
            dst_ref=occ_in.at[d - 1],
            send_sem=occ_sem.at[0],
            recv_sem=occ_sem.at[1],
            device_id=(g, (band + d) % nband),
            device_id_type=MESH,
        ).start()
    wait_bytes(occ_in, occ_sem.at[1])
    occ = occ_mine[...]
    for d in range(nband - 1):
        occ = occ + occ_in[d]

    u = orb[2 * ORB_REACH + 1 : 2 * ORB_REACH + 2, :]
    potential = []
    for k in range(-ORB_REACH, ORB_REACH + 1):
        value = occ[abs(k) : abs(k) + 1, :]
        value = ahead(value, k) if k < 0 else value
        same = orb[ORB_REACH + k : ORB_REACH + k + 1, :]
        potential.append(u * ((0.5 if k == 0 else 0.0) - value * same) * same)

    for h in halves:
        mixed = []
        for i in range(rows // 8):
            x = pot[h * rows + i * 8 : h * rows + i * 8 + 8, :]
            total = potential[ORB_REACH] * x
            for k in range(-ORB_REACH, ORB_REACH + 1):
                if k != 0:
                    total = total + potential[ORB_REACH + k] * ahead(x, k)
            mixed.append(total)
        for cols, value in times_ortho(jnp.concatenate(mixed, axis=0), h):
            half_o[part[h], cols] = value.astype(BF16)
        for j in range(npw // block):
            cols = pl.ds(j * block, block)
            value = dot_nt(half_o[part[h], :], atom[cols, :])
            hw[part[h], cols] = value
            cpsi[part[h], cols] = value.astype(BF16)
        for j in range(nbeta // step):
            cols = pl.ds(j * step, step)
            wb[1, part[h], cols] = dot_nn(cpsi[part[h], :], beta[:, cols])
        sums[2][h].start()

    middle(2)
    for h in halves:
        sums[2][h].finish()
        apply_q(fb.at[1], h)
        for j in range(npw // block):
            cols = pl.ds(j * block, block)
            value = hw[part[h], cols] + dot_nt(half_b[part[h], :], beta[cols, :])
            out[part[h], cols] = value.astype(BF16)

    for w in range(3):
        for h in halves:
            sums[w][h].drain()
    wait_bytes(occ_in, occ_sem.at[0])


def shards(
    band_coeffs, beta_vectors, atomic_waves, beta_coupling, ortho_inverse, hubbard_energy, band_weight, orbital_start,
    orbital_species, beta_start,
):
    npw, bands = band_coeffs.shape
    nbeta, norb = beta_vectors.shape[1], atomic_waves.shape[1]
    rows = bands // HALVES
    wide_b, wide_o = nbeta * rows // (NY * 8), norb * rows // (NY * 8)
    hbm = pl.BlockSpec(memory_space=pl.ANY)
    vmem = pl.BlockSpec(memory_space=pltpu.VMEM)
    smem = pl.BlockSpec(memory_space=pltpu.SMEM)
    out = pl.pallas_call(
        kernel,
        out_shape=jax.ShapeDtypeStruct((bands, npw), BF16),
        in_specs=[hbm, hbm, hbm, hbm, vmem, smem, vmem, vmem, vmem, vmem],
        out_specs=vmem,
        scratch_shapes=[
            pltpu.VMEM((bands, npw), BF16),
            pltpu.VMEM((npw, nbeta), BF16),
            pltpu.VMEM((npw, norb), BF16),
            pltpu.VMEM((norb, norb), BF16),
            pltpu.VMEM((16, nbeta), F32),
            pltpu.VMEM((16, norb), F32),
            pltpu.VMEM((bands, 1), F32),
            pltpu.VMEM((2, bands, nbeta), F32),
            pltpu.VMEM((bands, norb), F32),
            pltpu.VMEM((2, bands, nbeta), F32),
            pltpu.VMEM((bands, norb), F32),
            pltpu.VMEM((bands, nbeta), BF16),
            pltpu.VMEM((bands, norb), BF16),
            pltpu.VMEM((bands, npw), F32),
            pltpu.VMEM((bands, npw), BF16),
            pltpu.VMEM((bands, norb), F32),
            pltpu.VMEM((8, norb), F32),
            pltpu.VMEM((7, 8, norb), F32),
            pltpu.VMEM((2 * HALVES, NY - 1, 8, wide_b), F32),
            pltpu.VMEM((HALVES, NY - 1, 8, wide_o), F32),
            pltpu.VMEM((3 * HALVES, NZ - 1, 8, 128), F32),
            pltpu.VMEM((2 * HALVES, 8, wide_b), F32),
            pltpu.VMEM((HALVES, 8, wide_o), F32),
            pltpu.SemaphoreType.DMA((7,)),
            pltpu.SemaphoreType.DMA((3 * HALVES, 4)),
            pltpu.SemaphoreType.DMA((3 * HALVES, 4)),
            pltpu.SemaphoreType.DMA((2,)),
        ],
        compiler_params=pltpu.CompilerParams(
            collective_id=0, has_side_effects=True, vmem_limit_bytes=48 * 2**20
        ),
        name="hubbard",
    )(
        band_coeffs.T,
        beta_vectors,
        atomic_waves,
        ortho_inverse,
        beta_coupling.T,
        hubbard_energy[None, :],
        band_weight[None, :],
        orbital_start[None, :],
        orbital_species[None, :],
        beta_start[None, :],
    )
    return out.T


def solution(mesh):
    placed = (
        P("ga", "band"), P("ga", None), P("ga", None), P(), P(), P(), P("band"), P(), P(), P(),
    )
    return jax.shard_map(shards, mesh=mesh, in_specs=placed, out_specs=P("ga", "band"), check_vma=False)
```

time: 894 us -> 154 us (0.17)
  waiting for transfers between devices: 818 us -> 0 us
  Pallas kernels: 0 us -> 144 us
  matrix products: 35 us -> 0 us
  blocking collectives: 21.6 us -> 0 us
  between operations: 13.6 us -> 0.02 us
    psum x3 -> x0, waiting for transfers between devices: 818 us -> none  [the longest x1 281 us: shards(): lax.psum(jnp.dot(beta_vectors.T, band_coeffs, preferred_element_type=jnp....]
    pallas_call x0 -> x1, Pallas kernels: none -> 144 us  [shards(): pl.pallas_call(kernel, out_shape=jax.ShapeDtypeStruct((bands, npw), BF16)...]
    dot_general x8 -> x0, matrix products: 35 us -> none  [the longest x1 8.77 us: shards(): jnp.dot(atomic_waves.T, correlation_psi, preferred_element_type=jnp.float32)]
    psum x1 -> x0, blocking collectives: 21.6 us -> none  [shards(): lax.psum(occupancy(extended, band_weight, mask, ORB_REACH, norbit), 'band')]
  transfers between devices with their start and end apart: 3 -> 0, of which waited for: 3 -> 0; matrix products, arithmetic and copies ran while one was open for 0% -> 0% of each run, Pallas kernels for 0% -> 0%
where the time goes in v1:
time: 154 us; the launch traced here: 152 us
  Pallas kernels  144 us (94%)
  local copies, waits for them, and re-layouts  7.61 us (5%)
    pallas_call x1, Pallas kernels, shards(): pl.pallas_call(kernel, out_shape=jax.ShapeDtypeStruct((bands, npw), BF16)...  144 us
    unnamed x13, local copies, waits for them, and re-layouts  6.21 us

profile of v1, /device:TPU:6, one launch (start us, length us, event | category | flops | bytes accessed | tf_op | source)
XLA Modules:
  0.0 151.7 jit_solution(6681266727709127104)
XLA Ops:
  0.0 0.7 broadcast_in_dim.17.ostart
  0.7 0.7 broadcast_in_dim.18.ospec
  1.4 0.0 copy-start
  1.4 1.7 %copy-done = bf16[1024,1280]{1,0:T(8,128)(2,1)S(1)} copy-done((bf16[1024,1280]{1,0:T(8,128)(2,1)S(1)}, bf16[1024,1280]{1,0:T(8,128)(2,1)}, u32[]{:S(2)}) %copy-start) | copy-done | bytes 2621464
  3.1 0.0 copy-start.1
  3.1 0.9 copy-done.1
  4.0 0.0 copy-start.2
  4.0 0.9 copy-done.2
  5.0 0.0 copy-start.3
  5.0 0.7 copy-done.3
  5.7 0.0 copy-start.4
  5.7 0.7 copy-done.4
  6.3 0.0 copy-start.5
  6.3 0.7 copy-done.5
  7.0 144.0 %hubbard.1 = bf16[64,1024]{1,0:T(8,128)(2,1)S(1)} custom-call(bf16[64,1024]{1,0:T(8,128)(2,1)S(1)} %bitcast.7, bf16[1024,2048]{1,0:T(8,128)(2,1)} %beta_hbm.1, bf16[1024,1280]{1,0:T(8,128)(2,1)S(1)} %copy-done, bf16[1280,1280]{1,0:T(8,128)(2,1)} %ortho_hbm.1, f32[11,2048]{1,0:T(8,128)S(1)} %bitcast.8, f32[1,3]{1,0:T(1,128)S(1)} %bitcast.10, ...), custom_call_target="tpu_custom_call" | custom-call | tf_op jit(solution)/shard_map/hubbard/pallas_call | solution.py:366
  151.0 0.7 copy.12
Async XLA Ops:
  1.4 1.7 %copy-start = (bf16[1024,1280]{1,0:T(8,128)(2,1)S(1)}, bf16[1024,1280]{1,0:T(8,128)(2,1)}, u32[]{:S(2)}) copy-start(bf16[1024,1280]{1,0:T(8,128)(2,1)} %atom_hbm.1) | copy-start | bytes 7864324
  3.1 0.9 copy-start.1
  4.0 0.9 copy-start.2
  5.0 0.7 copy-start.3
  5.7 0.7 copy-start.4
  6.3 0.7 copy-start.5

commit v2 on v1

v2 whole, which is shorter than its diff:
```python
import functools

import jax
import jax.numpy as jnp
from jax import lax
from jax.experimental import pallas as pl
from jax.experimental.pallas import tpu as pltpu
from jax.sharding import PartitionSpec as P

ORB_REACH = 4
BETA_REACH = 5
NY = 8
NZ = 16
CROSS_B = 2
CROSS_O = 2
MESH = pl.DeviceIdType.MESH
F32 = jnp.float32
BF16 = jnp.bfloat16


def dot_nn(a, b):
    return jnp.dot(a, b, preferred_element_type=F32)


def dot_nt(a, b):
    return lax.dot_general(a, b, (((1,), (1,)), ((), ())), preferred_element_type=F32)


def ahead(x, k):
    n = x.shape[1]
    return x if k % n == 0 else pltpu.roll(x, (-k) % n, 1)


def order(n):
    return sorted(range(1, n), key=lambda d: -min(d, n - d))


def wait_bytes(ref, sem):
    pltpu.make_async_copy(ref, ref, sem).wait()


class CrossSum:
    def __init__(self, src, dst, z_in, y_in, mine, sems, y, z, band):
        self.src, self.dst = src, dst
        self.z_in, self.y_in, self.mine = z_in, y_in, mine
        self.width = z_in.shape[2]
        self.tiles = self.width // 128
        self.base = src.shape[1] - 2 * self.width
        self.in_z, self.in_y, self.out_y, self.out_z = (sems[0].at[p] for p in range(4))
        self.sent = sems[1]
        self.y, self.z, self.band = y, z, band
        self.owners = [t * NY // self.tiles for t in range(self.tiles)]

    def place(self, z):
        rows = pl.ds(pl.multiple_of((z // 2) * 8, 8), 8)
        return rows, pl.ds(pl.multiple_of(self.base + (z % 2) * self.width, 128), self.width)

    def tile(self, t):
        rows, _ = self.place(self.z)
        return rows, pl.ds(pl.multiple_of(self.base + (self.z % 2) * self.width + t * 128, 128), 128)

    def copy(self, src, dst, recv, phase, y, z):
        pltpu.make_async_remote_copy(
            src_ref=src,
            dst_ref=dst,
            send_sem=self.sent.at[phase],
            recv_sem=recv,
            device_id=(y * NZ + z, self.band),
            device_id_type=MESH,
        ).start()

    def start(self):
        for d in order(NZ):
            to = (self.z + d) % NZ
            self.copy(self.src.at[self.place(to)], self.z_in.at[d - 1], self.in_z, 0, self.y, to)

    def sum_z(self):
        wait_bytes(self.z_in, self.in_z)
        total = self.src[self.place(self.z)]
        for d in range(NZ - 1):
            total = total + self.z_in[d]
        self.mine[...] = total
        for t, owner in enumerate(self.owners):

            def go(t=t, owner=owner):
                slot = (owner - self.y + NY) % NY - 1
                self.copy(self.mine.at[:, pl.ds(t * 128, 128)], self.y_in.at[slot], self.in_y, 1, owner, self.z)

            pl.when(self.y != owner)(go)

    def sum_y(self):
        for t, owner in enumerate(self.owners):

            def go(t=t):
                wait_bytes(self.y_in, self.in_y)
                total = self.mine[:, t * 128 : t * 128 + 128]
                for d in range(NY - 1):
                    total = total + self.y_in[d]
                here = self.tile(t)
                self.dst[here] = total
                at = self.dst.at[here]
                for d in order(NY):
                    self.copy(at, at, self.out_y, 2, (self.y + d) % NY, self.z)

            pl.when(self.y == owner)(go)

    def others(self, sem):
        owns = self.y == self.owners[0]
        for owner in self.owners[1:]:
            owns = jnp.logical_or(owns, self.y == owner)
        pl.when(owns)(lambda: wait_bytes(self.y_in.at[pl.ds(0, self.tiles - 1)], sem))
        pl.when(jnp.logical_not(owns))(lambda: wait_bytes(self.y_in.at[pl.ds(0, self.tiles)], sem))
        return owns

    def spread(self):
        self.others(self.out_y)
        at = self.dst.at[self.place(self.z)]
        for d in order(NZ):
            self.copy(at, at, self.out_z, 3, self.y, (self.z + d) % NZ)

    def finish(self):
        wait_bytes(self.z_in, self.out_z)

    def drain(self):
        wait_bytes(self.z_in, self.sent.at[0])
        owns = self.others(self.sent.at[1])
        pl.when(owns)(lambda: wait_bytes(self.y_in, self.sent.at[2]))
        wait_bytes(self.z_in, self.sent.at[3])


class RingSum:
    def __init__(self, src, dst, y_in, z_in, mine, sems, y, z, band):
        self.src, self.dst = src, dst
        self.pairs = y_in.shape[0]
        self.stride = NZ // self.pairs
        self.y_in, self.z_in, self.mine = y_in, z_in, mine
        self.in_y, self.in_z, self.out_z, self.out_y, self.sent = sems
        self.y, self.z, self.band = y, z, band
        self.home = (z // self.stride) % self.pairs
        near = sorted(range(self.pairs), key=lambda d: min(d, self.pairs - d))
        self.near = [(self.home + d) % self.pairs for d in near]
        self.rows = pl.ds(pl.multiple_of(y * 8, 8), 8)
        self.side = z % self.stride
        self.every = self.stride * self.pairs == NZ
        self.owner = jnp.logical_and(self.side < 2, z // self.stride < self.pairs)

    def lanes(self, pair):
        return pl.ds(pl.multiple_of(pair * 256, 256), 256)

    def tile(self, pair, side):
        return pl.ds(pl.multiple_of(pair * 256 + side * 128, 128), 128)

    def copy(self, src, dst, recv, phase, y, z):
        pltpu.make_async_remote_copy(
            src_ref=src,
            dst_ref=dst,
            send_sem=self.sent.at[phase],
            recv_sem=recv,
            device_id=(y * NZ + z, self.band),
            device_id_type=MESH,
        ).start()

    def when(self, cond, body):
        if self.every:
            body()
        else:
            pl.when(cond)(body)

    def unless(self, cond, body):
        if not self.every:
            pl.when(jnp.logical_not(cond))(body)

    def start(self, i):
        pair = self.near[self.pairs - 1 - i]
        for d in order(NY):
            to = (self.y + d) % NY
            rows = pl.ds(pl.multiple_of(to * 8, 8), 8)
            self.copy(self.src.at[rows, self.lanes(pair)], self.y_in.at[pair, d - 1], self.in_y.at[pair], 0, to, self.z)

    def sum_in(self):
        for i in range(self.pairs):
            pair = self.near[self.pairs - 1 - i]
            wait_bytes(self.y_in.at[pair], self.in_y.at[pair])
            total = self.src[self.rows, self.lanes(pair)]
            for d in range(NY - 1):
                total = total + self.y_in[pair, d]
            self.mine[:, self.lanes(pair)] = total
            for side in range(2):
                to = pair * self.stride + side

                def go(to=to, side=side, pair=pair):
                    gap = (to - self.z + NZ) % NZ - 1
                    self.copy(self.mine.at[:, self.tile(pair, side)], self.z_in.at[gap], self.in_z, 1, self.y, to)

                if i < self.pairs - 1 and self.every:
                    go()
                else:
                    pl.when(to != self.z)(go)

    def sum_out(self):
        def go():
            wait_bytes(self.z_in, self.in_z)
            here = self.tile(self.home, self.side)
            total = self.mine[:, here]
            for d in range(NZ - 1):
                total = total + self.z_in[d]
            self.dst[self.rows, here] = total
            at = self.dst.at[self.rows, here]
            for d in order(NZ):
                self.copy(at, at, self.out_z.at[self.home], 2, self.y, (self.z + d) % NZ)

        self.when(self.owner, go)

    def spread(self, low, high):
        for i in range(low, high):
            pair = self.near[i]
            sem = self.out_z.at[pair]
            at = self.dst.at[self.rows, self.lanes(pair)]
            if i == 0:
                self.when(self.owner, lambda: wait_bytes(self.z_in.at[0], sem))
                self.unless(self.owner, lambda: wait_bytes(self.z_in.at[pl.ds(0, 2)], sem))
            else:
                wait_bytes(self.z_in.at[pl.ds(0, 2)], sem)
            for d in order(NY):
                self.copy(at, at, self.out_y, 3, (self.y + d) % NY, self.z)

    def finish(self):
        wait_bytes(self.y_in, self.out_y)

    def drain(self):
        tiles = 2 * self.pairs
        wait_bytes(self.y_in, self.sent.at[0])
        if self.every:
            wait_bytes(self.z_in, self.sent.at[1])
        else:
            own = self.owner
            pl.when(own)(lambda: wait_bytes(self.z_in.at[pl.ds(0, tiles - 1)], self.sent.at[1]))
            pl.when(jnp.logical_not(own))(lambda: wait_bytes(self.z_in.at[pl.ds(0, tiles)], self.sent.at[1]))
        self.when(self.owner, lambda: wait_bytes(self.z_in, self.sent.at[2]))
        wait_bytes(self.y_in, self.sent.at[3])


def split3(x):
    high = x.astype(BF16)
    rest = x - high.astype(F32)
    mid = rest.astype(BF16)
    low = (rest - mid.astype(F32)).astype(BF16)
    return jnp.concatenate([high, mid, low], axis=0)


def kernel(
    psi_hbm, beta_hbm, atom_hbm, ortho_hbm, coup_hbm, energy_hbm, weight_hbm, ostart_hbm, ospec_hbm, bstart_hbm, out,
    psi, beta, atom, ortho, coup_in, energy, weight_in, ostart, ospec, bstart, coup, orb, wcol, wb, wo, fb, fo, half_b,
    half_o, hw, cpsi, pot, occ_mine, occ_in, yb_in, yo_in, z_in, mine_b, mine_o, xzb_in, xzo_in, xy_in, xmine_b, xmine_o,
    load_sem, piece_sem, in_y, in_z, out_z, out_y, sent, cross_in, cross_sent, occ_sem,
):
    bands, npw = psi.shape
    nbeta, norb = beta.shape[1], atom.shape[1]
    g = lax.axis_index("ga")
    band = lax.axis_index("band")
    y, z = g // NZ, g % NZ
    nband = 8

    def ring(which):
        if which == 1:
            src, dst, y_in, mine = wo, fo, yo_in, mine_o
        else:
            n = which // 2
            src, dst, y_in, mine = wb.at[n], fb.at[n], yb_in.at[n], mine_b.at[n]
        sems = (in_y.at[which], in_z.at[which], out_z.at[which], out_y.at[which], sent.at[which])
        x_in, x_mine = (xzo_in, xmine_o) if which == 1 else (xzb_in.at[which // 2], xmine_b.at[which // 2])
        x_sems = (cross_in.at[which], cross_sent.at[which])
        return (
            RingSum(src, dst, y_in, z_in.at[which], mine, sems, y, z, band),
            CrossSum(src, dst, x_in, xy_in.at[which], x_mine, x_sems, y, z, band),
        )

    (first_sum, first_cross), (second_sum, second_cross), (third_sum, third_cross) = ring(0), ring(1), ring(2)

    def carry(one, cross):
        one.sum_in()
        cross.sum_z()
        one.sum_out()
        cross.sum_y()
        one.spread(0, 1)
        cross.spread()
        one.spread(1, one.pairs)

    def pieces(one, cross):
        for first in range(cross.base, cross.base + 2 * cross.width, 256):
            yield pl.ds(first, 256), None
        for i in range(one.pairs):
            yield one.lanes(one.near[one.pairs - 1 - i]), i

    def begin(one, cross, i):
        if i is not None:
            if i == 0:
                cross.start()
            one.start(i)

    psi_load = pltpu.make_async_copy(psi_hbm, psi, load_sem.at[0])
    psi_load.start()
    beta_loads = []
    for n, (cols, _) in enumerate(pieces(first_sum, first_cross)):
        beta_loads.append(pltpu.make_async_copy(beta_hbm.at[:, cols], beta.at[:, cols], piece_sem.at[n]))
    pairs = [
        (coup_hbm, coup_in), (energy_hbm, energy), (weight_hbm, weight_in), (ostart_hbm, ostart), (ospec_hbm, ospec),
        (bstart_hbm, bstart), (atom_hbm, atom), (ortho_hbm, ortho),
    ]
    late = [pltpu.make_async_copy(a, b, load_sem.at[1 + i]) for i, (a, b) in enumerate(pairs)]
    for c in beta_loads + late:
        c.start()

    barrier = pltpu.get_barrier_semaphore()
    for d in order(NZ):
        pl.semaphore_signal(barrier, inc=1, device_id=(y * NZ + (z + d) % NZ, band), device_id_type=MESH)
    for d in order(NY):
        pl.semaphore_signal(barrier, inc=1, device_id=(((y + d) % NY) * NZ + z, band), device_id_type=MESH)
    for d in range(1, nband):
        pl.semaphore_signal(barrier, inc=1, device_id=(g, (band + d) % nband), device_id_type=MESH)

    psi_load.wait()
    for n, (cols, i) in enumerate(pieces(first_sum, first_cross)):
        beta_loads[n].wait()
        wb[0, :, cols] = dot_nn(psi[...], beta[:, cols])
        if i == 0:
            pl.semaphore_wait(barrier, NZ - 1 + NY - 1 + nband - 1)
        begin(first_sum, first_cross, i)

    for c in late:
        c.wait()
    place = lax.broadcasted_iota(jnp.int32, (1, nbeta), 1)
    first = bstart[...].reshape(1, nbeta)
    for k in range(-BETA_REACH, BETA_REACH + 1):
        there = jnp.logical_and(place + k >= 0, place + k < nbeta)
        same = jnp.logical_and(ahead(first, k) == first, there)
        mirror = ahead(coup_in[BETA_REACH - k : BETA_REACH - k + 1, :], k)
        value = 0.5 * (coup_in[BETA_REACH + k : BETA_REACH + k + 1, :] + mirror)
        coup[BETA_REACH + k : BETA_REACH + k + 1, :] = jnp.where(same, value, 0.0)
    place = lax.broadcasted_iota(jnp.int32, (1, norb), 1)
    first = ostart[...].reshape(1, norb)
    for k in range(-ORB_REACH, ORB_REACH + 1):
        there = jnp.logical_and(place + k >= 0, place + k < norb)
        same = jnp.logical_and(ahead(first, k) == first, there)
        orb[ORB_REACH + k : ORB_REACH + k + 1, :] = jnp.where(same, 1.0, 0.0)
    species = ospec[...].reshape(1, norb)
    u = jnp.zeros((1, norb), F32)
    for s in range(3):
        u = u + jnp.where(species == s, energy[s], 0.0)
    orb[2 * ORB_REACH + 1 : 2 * ORB_REACH + 2, :] = u
    row = lax.broadcasted_iota(jnp.int32, (bands, bands), 0)
    col = lax.broadcasted_iota(jnp.int32, (bands, bands), 1)
    wcol[...] = jnp.sum(jnp.where(row == col, weight_in[...].reshape(1, bands), 0.0), axis=1, keepdims=True)

    def apply_q(full):
        for i in range(bands // 16):
            pair = []
            for j in range(2):
                x = full[i * 16 + j * 8 : i * 16 + j * 8 + 8, :]
                total = coup[BETA_REACH : BETA_REACH + 1, :] * x
                for k in range(-BETA_REACH, BETA_REACH + 1):
                    if k != 0:
                        total = total + coup[BETA_REACH + k : BETA_REACH + k + 1, :] * ahead(x, k)
                pair.append(total)
            half_b[i * 16 : i * 16 + 16, :] = jnp.concatenate(pair, axis=0).astype(BF16)

    block = 256

    carry(first_sum, first_cross)
    first_sum.finish()
    first_cross.finish()
    apply_q(fb.at[0])
    for j in range(npw // block):
        cols = pl.ds(j * block, block)
        value = psi[:, cols].astype(F32) + dot_nt(half_b[...], beta[cols, :])
        cpsi[:, cols] = value.astype(BF16)
    for cols, i in pieces(second_sum, second_cross):
        wo[:, cols] = dot_nn(cpsi[...], atom[:, cols])
        begin(second_sum, second_cross, i)
    carry(second_sum, second_cross)

    def times_ortho(x):
        stacked = split3(x)
        for j in range(norb // block):
            cols = pl.ds(j * block, block)
            y3 = dot_nt(stacked, ortho[cols, :])
            yield cols, y3[:bands] + y3[bands : 2 * bands] + y3[2 * bands :]

    second_sum.finish()
    second_cross.finish()
    for cols, value in times_ortho(fo[...]):
        pot[:, cols] = value
    accs = None
    for i in range(bands // 8):
        p = pot[i * 8 : i * 8 + 8, :]
        weighted = p * wcol[i * 8 : i * 8 + 8, :]
        terms = [weighted * ahead(p, k) for k in range(ORB_REACH + 1)]
        accs = terms if accs is None else [a + t for a, t in zip(accs, terms)]
    for k in range(ORB_REACH + 1):
        occ_mine[k : k + 1, :] = jnp.sum(accs[k], axis=0, keepdims=True)
    occ_mine[ORB_REACH + 1 :, :] = jnp.zeros((8 - ORB_REACH - 1, norb), F32)
    for d in range(1, nband):
        pltpu.make_async_remote_copy(
            src_ref=occ_mine,
            dst_ref=occ_in.at[d - 1],
            send_sem=occ_sem.at[0],
            recv_sem=occ_sem.at[1],
            device_id=(g, (band + d) % nband),
            device_id_type=MESH,
        ).start()
    wait_bytes(occ_in, occ_sem.at[1])
    occ = occ_mine[...]
    for d in range(nband - 1):
        occ = occ + occ_in[d]

    u = orb[2 * ORB_REACH + 1 : 2 * ORB_REACH + 2, :]
    potential = []
    for k in range(-ORB_REACH, ORB_REACH + 1):
        value = occ[abs(k) : abs(k) + 1, :]
        value = ahead(value, k) if k < 0 else value
        same = orb[ORB_REACH + k : ORB_REACH + k + 1, :]
        potential.append(u * ((0.5 if k == 0 else 0.0) - value * same) * same)

    mixed = []
    for i in range(bands // 8):
        x = pot[i * 8 : i * 8 + 8, :]
        total = potential[ORB_REACH] * x
        for k in range(-ORB_REACH, ORB_REACH + 1):
            if k != 0:
                total = total + potential[ORB_REACH + k] * ahead(x, k)
        mixed.append(total)
    for cols, value in times_ortho(jnp.concatenate(mixed, axis=0)):
        half_o[:, cols] = value.astype(BF16)
    for j in range(npw // block):
        cols = pl.ds(j * block, block)
        value = dot_nt(half_o[...], atom[cols, :])
        hw[:, cols] = value
        cpsi[:, cols] = value.astype(BF16)
    for cols, i in pieces(third_sum, third_cross):
        wb[1, :, cols] = dot_nn(cpsi[...], beta[:, cols])
        begin(third_sum, third_cross, i)
    carry(third_sum, third_cross)
    third_sum.finish()
    third_cross.finish()
    apply_q(fb.at[1])
    for j in range(npw // block):
        cols = pl.ds(j * block, block)
        value = hw[:, cols] + dot_nt(half_b[...], beta[cols, :])
        out[:, cols] = value.astype(BF16)

    for s in (first_sum, first_cross, second_sum, second_cross, third_sum, third_cross):
        s.drain()
    wait_bytes(occ_in, occ_sem.at[0])


def shards(
    band_coeffs, beta_vectors, atomic_waves, beta_coupling, ortho_inverse, hubbard_energy, band_weight, orbital_start,
    orbital_species, beta_start,
):
    npw, bands = band_coeffs.shape
    nbeta, norb = beta_vectors.shape[1], atomic_waves.shape[1]
    hbm = pl.BlockSpec(memory_space=pl.ANY)
    vmem = pl.BlockSpec(memory_space=pltpu.VMEM)
    out = pl.pallas_call(
        kernel,
        out_shape=jax.ShapeDtypeStruct((bands, npw), BF16),
        in_specs=[hbm] * 10,
        out_specs=vmem,
        scratch_shapes=[
            pltpu.VMEM((bands, npw), BF16),
            pltpu.VMEM((npw, nbeta), BF16),
            pltpu.VMEM((npw, norb), BF16),
            pltpu.VMEM((norb, norb), BF16),
            pltpu.VMEM(beta_coupling.shape[::-1], F32),
            pltpu.SMEM(hubbard_energy.shape, F32),
            pltpu.VMEM((bands,), F32),
            pltpu.VMEM((norb,), jnp.int32),
            pltpu.VMEM((norb,), jnp.int32),
            pltpu.VMEM((nbeta,), jnp.int32),
            pltpu.VMEM((16, nbeta), F32),
            pltpu.VMEM((16, norb), F32),
            pltpu.VMEM((bands, 1), F32),
            pltpu.VMEM((2, bands, nbeta), F32),
            pltpu.VMEM((bands, norb), F32),
            pltpu.VMEM((2, bands, nbeta), F32),
            pltpu.VMEM((bands, norb), F32),
            pltpu.VMEM((bands, nbeta), BF16),
            pltpu.VMEM((bands, norb), BF16),
            pltpu.VMEM((bands, npw), F32),
            pltpu.VMEM((bands, npw), BF16),
            pltpu.VMEM((bands, norb), F32),
            pltpu.VMEM((8, norb), F32),
            pltpu.VMEM((7, 8, norb), F32),
            pltpu.VMEM((2, nbeta // 256 - CROSS_B, NY - 1, 8, 256), F32),
            pltpu.VMEM((norb // 256 - CROSS_O, NY - 1, 8, 256), F32),
            pltpu.VMEM((3, NZ - 1, 8, 128), F32),
            pltpu.VMEM((2, 8, nbeta), F32),
            pltpu.VMEM((8, norb), F32),
            pltpu.VMEM((2, NZ - 1, 8, 128 * CROSS_B), F32),
            pltpu.VMEM((NZ - 1, 8, 128 * CROSS_O), F32),
            pltpu.VMEM((3, NY - 1, 8, 128), F32),
            pltpu.VMEM((2, 8, 128 * CROSS_B), F32),
            pltpu.VMEM((8, 128 * CROSS_O), F32),
            pltpu.SemaphoreType.DMA((9,)),
            pltpu.SemaphoreType.DMA((nbeta // 256,)),
            pltpu.SemaphoreType.DMA((3, nbeta // 256)),
            pltpu.SemaphoreType.DMA((3,)),
            pltpu.SemaphoreType.DMA((3, nbeta // 256)),
            pltpu.SemaphoreType.DMA((3,)),
            pltpu.SemaphoreType.DMA((3, 4)),
            pltpu.SemaphoreType.DMA((3, 4)),
            pltpu.SemaphoreType.DMA((3, 4)),
            pltpu.SemaphoreType.DMA((2,)),
        ],
        compiler_params=pltpu.CompilerParams(
            collective_id=0, has_side_effects=True, vmem_limit_bytes=60 * 2**20
        ),
        name="hubbard",
    )(
        band_coeffs.T,
        beta_vectors,
        atomic_waves,
        ortho_inverse,
        beta_coupling.T,
        hubbard_energy,
        band_weight,
        orbital_start,
        orbital_species,
        beta_start,
    )
    return out.T


def solution(mesh):
    placed = (
        P("ga", "band"), P("ga", None), P("ga", None), P(), P(), P(), P("band"), P(), P(), P(),
    )
    return jax.shard_map(shards, mesh=mesh, in_specs=placed, out_specs=P("ga", "band"), check_vma=False)
```

time: 154 us -> 126 us (0.82)
  Pallas kernels: 144 us -> 123 us
  local copies, waits for them, and re-layouts: 7.61 us -> 1.57 us
    pallas_call x1, Pallas kernels: 144 us -> 123 us  [shards(): pl.pallas_call(kernel, out_shape=jax.ShapeDtypeStruct((bands, npw), BF16)...]
    unnamed x13 -> x1, local copies, waits for them, and re-layouts: 6.21 us -> 1.57 us
where the time goes in v2:
time: 126 us; the launch traced here: 124 us
  Pallas kernels  123 us (98%)
  local copies, waits for them, and re-layouts  1.57 us (1%)
    pallas_call x1, Pallas kernels, shards(): pl.pallas_call(kernel, out_shape=jax.ShapeDtypeStruct((bands, npw), BF16)...  123 us

profile of v2, /device:TPU:6, one launch (start us, length us, event | category | flops | bytes accessed | tf_op | source)
XLA Modules:
  0.0 124.2 jit_solution(16857433951697124459)
XLA Ops:
  0.0 122.6 %hubbard.1 = bf16[64,1024]{1,0:T(8,128)(2,1)} custom-call(bf16[64,1024]{1,0:T(8,128)(2,1)} %bitcast.4, bf16[1024,2048]{1,0:T(8,128)(2,1)} %beta_hbm.1, bf16[1024,1280]{1,0:T(8,128)(2,1)} %atom_hbm.1, bf16[1280,1280]{1,0:T(8,128)(2,1)} %ortho_hbm.1, f32[11,2048]{1,0:T(8,128)} %bitcast.5, f32[3]{0:T(128)} %energy_hbm.1, f32[64]{0:T(128)} %weight_hbm.1, ...), custom_call_target="tpu_custom_call" | custom-call | tf_op jit(solution)/shard_map/hubbard/pallas_call | solution.py:464
  122.6 1.6 %copy.12 = bf16[1024,64]{0,1:T(8,128)(2,1)} copy(bf16[1024,64]{0,1:T(8,128)(2,1)} %bitcast.3) | data formatting | bytes 262144
